TPU v7x, 32 devices: a whole 2x2x4 slice. The times are simulated.
32 devices in a mesh: row: 4 (over x, core), col: 2 (over y), tm: 4 (over z).
Axes of the slice: x: 2, y: 2, z: 4, core: 2. Of those that a mesh axis runs over, the one named last changes fastest.
Arguments:
- right_sides: bfloat16 [8, 256, 16384], P(None, 'tm', ('row', 'col')), may hold values from -6 to 6
- eigen_basis: bfloat16 [16384, 16384], P('row', 'col'), may hold values from -0.046875 to 0.046875
- space_values: float32 [16384], P('col'), may hold values from 0.02 to 4
- time_basis: bfloat16 [256, 256], replicated, may hold values from -0.375 to 0.375
- time_values: float32 [256], replicated, may hold values from 0.05 to 4
- noise_level: float32 [1], replicated, may hold values from 0.05 to 0.5
Outputs:
- solved: float32 [8, 256, 16384], P(None, 'tm', ('row', 'col'))
All inputs are finite; a program needn't handle non-finite values.
Results may differ from a plain program's by a relative error of at most 0.0037.
Values may be sent and summed in bfloat16 or wider, within the bound.
A program may use at most 192 MiB of HBM per device.

v0:
```python
import jax
import jax.numpy as jnp
from jax import lax
from jax.sharding import PartitionSpec as P


def shards(right_sides, eigen_basis, space_values, time_basis, time_values, noise_level):
    span = space_values.shape[0] // lax.axis_size("tm")
    value_part = lax.dynamic_slice_in_dim(space_values, lax.axis_index("tm") * span, span, 0)
    partial_value = jnp.einsum(
        "rts,si->rti",
        lax.all_gather(right_sides, "col", axis=2, tiled=True),
        eigen_basis,
        preferred_element_type=jnp.float32,
    )
    spectral = lax.psum(partial_value, "row").astype(jnp.bfloat16)
    mixed = jnp.einsum(
        "tj,kti->kji",
        time_basis,
        lax.all_to_all(spectral, "tm", split_axis=2, concat_axis=1, tiled=True),
        preferred_element_type=jnp.float32,
    )
    denom = value_part[None, None, :] * time_values[None, :, None] + noise_level[0]
    scaled = (mixed / denom).astype(jnp.bfloat16)
    own_part = lax.all_to_all(
        jnp.einsum("tj,kji->kti", time_basis, scaled, preferred_element_type=jnp.float32).astype(
            jnp.bfloat16
        ),
        "tm",
        split_axis=1,
        concat_axis=2,
        tiled=True,
    )
    terms = jnp.einsum("rti,si->rts", own_part, eigen_basis, preferred_element_type=jnp.float32)
    return lax.psum_scatter(terms, "col", scatter_dimension=2, tiled=True)


def solution(mesh):
    placed = (P(None, "tm", ("row", "col")), P("row", "col"), P("col"), P(), P(), P())
    return jax.shard_map(
        shards, mesh=mesh, in_specs=placed, out_specs=P(None, "tm", ("row", "col")), check_vma=False
    )
```

profile of v0, /device:TPU:0, one launch (start us, length us, event | category | flops | bytes accessed | tf_op | source)
XLA Modules:
  0.0 1063.0 jit_solution(13978101292258448910)
XLA Ops:
  6.5 0.0 copy-start
  6.5 0.0 all-gather.2.cloned.1.call-start
  6.5 0.7 all-gather.2.cloned.1.call-update
  7.3 61.1 %all-gather.2.cloned.1.call-done = bf16[8,64,4096]{2,1,0:T(8,128)(2,1)} async-done(((bf16[8,64,2048]{2,1,0:T(8,128)(2,1)}), bf16[8,64,4096]{2,1,0:T(8,128)(2,1)}) %all-gather.2.cloned.1.call-update) | async-done | bytes 4194320 | tf_op jit(solution)/shard_map/all_gather | solution.py:12
  68.4 44.2 %fusion.2 = f32[8,64,8192]{2,1,0:T(8,128)} fusion(bf16[8,64,4096]{2,1,0:T(8,128)(2,1)} %all-gather.2.cloned.1.call-done, bf16[4096,8192]{1,0:T(8,128)(2,1)} %param.7), kind=kOutput, calls=%fused_computation.2 | convolution fusion | flops 34359738368 | bytes 88080384 | tf_op jit(solution)/shard_map/rts,si->rti/dot_general | solution.py:10
  112.6 287.5 %all-reduce.1 = bf16[8,64,8192]{2,1,0:T(8,128)(2,1)} all-reduce(f32[8,64,8192]{2,1,0:T(8,128)} %fusion.2), channel_id=1, replica_groups=mesh['row'=4,'col'=2,'tm'=4] {'row'}, use_global_device_ids=true, to_apply=%region_0.0 | all-reduce | flops 4194304 | bytes 25165824 | tf_op jit(solution)/shard_map/psum | solution.py:16
  400.1 18.7 %copy.16 = bf16[8,64,8192]{1,0,2:T(8,128)(2,1)} copy(bf16[8,64,8192]{2,1,0:T(8,128)(2,1)} %all-reduce.1) | data formatting | bytes 16777216 | tf_op jit(solution)/shard_map/convert_element_type | solution.py:16
  418.8 16.6 %reshape.36 = bf16[4,2,524288]{2,1,0:T(2,128)(2,1)} reshape(bf16[8192,8,64]{2,1,0:T(8,128)(2,1)} %bitcast.31) | data formatting | bytes 16777216
  435.4 0.0 copy-start.2
  435.4 5.8 all-to-all-start
  441.2 0.2 reduce-scatter.2.cloned.1.call-start
  442.1 0.7 dynamic_slice.3
  442.8 0.0 copy-done.2
  442.8 0.3 multiply_add_fusion
  443.1 182.0 %all-to-all-done = bf16[4,2,524288]{2,1,0:T(2,128)(2,1)} async-done(((bf16[4,2,524288]{2,1,0:T(2,128)(2,1)}), bf16[4,2,524288]{2,1,0:T(2,128)(2,1)}, u32[]{:S(2)}, u32[]{:S(2)}) %all-to-all-start) | async-done | bytes 8388640 | tf_op jit(solution)/shard_map/all_to_all | solution.py:20
  625.1 16.0 %reshape.37 = bf16[8192,8,64]{2,1,0:T(8,128)(2,1)} reshape(bf16[4,2,524288]{2,1,0:T(2,128)(2,1)} %all-to-all-done) | data formatting | bytes 16777216
  641.0 19.4 %copy.24 = bf16[8,64,4,2048]{3,2,1,0:T(4,128)(2,1)} copy(bf16[8,64,4,2048]{1,0,3,2:T(8,128)(2,1)} %bitcast.32) | data formatting | bytes 16777216 | tf_op jit(solution)/shard_map/all_to_all | solution.py:20
  660.5 11.5 %copy.18 = bf16[8,4,64,2048]{3,2,1,0:T(8,128)(2,1)} copy(bf16[8,4,64,2048]{3,1,2,0:T(4,128)(2,1)} %bitcast.33) | data formatting | bytes 16777216 | tf_op jit(solution)/shard_map/all_to_all | solution.py:20
  672.0 0.0 copy-done
  672.0 12.5 %convert_bitcast_fusion = bf16[8,256,2048]{1,2,0:T(8,128)(2,1)} fusion(f32[256,2048]{0,1:T(8,128)S(1)} %multiply_add_fusion, bf16[8,256,2048]{2,1,0:T(8,128)(2,1)} %bitcast.35, bf16[256,256]{1,0:T(8,128)(2,1)S(1)} %copy-done), kind=kOutput, calls=%fused_computation.6 | convolution fusion | flops 4307550208 | bytes 19005440 | tf_op jit(solution)/shard_map/tj,kji->kti/dot_general | solution.py:26
  684.5 12.5 %copy.20 = bf16[8,256,2048]{2,0,1:T(8,128)(2,1)} copy(bf16[8,256,2048]{1,2,0:T(8,128)(2,1)} %convert_bitcast_fusion) | data formatting | bytes 16777216 | tf_op jit(solution)/shard_map/convert_element_type | solution.py:26
  697.0 187.2 %all_to_all.36 = bf16[8,256,2048]{2,0,1:T(8,128)(2,1)S(1)} all-to-all(bf16[8,256,2048]{2,0,1:T(8,128)(2,1)} %copy.20), channel_id=1, replica_groups=mesh['row'=4,'col'=2,'tm'=4] {'tm'}, dimensions={1} | all-to-all | bytes 16777216 | tf_op jit(solution)/shard_map/all_to_all | solution.py:25
  884.1 17.4 %copy.22 = bf16[8,64,4,2048]{3,2,1,0:T(4,128)(2,1)} copy(bf16[8,64,4,2048]{3,0,1,2:T(8,128)(2,1)S(1)} %bitcast.34) | data formatting | bytes 16777216 | tf_op jit(solution)/shard_map/all_to_all | solution.py:25
  901.5 14.4 %all_to_all.33 = bf16[8,64,8192]{2,1,0:T(8,128)(2,1)} reshape(bf16[8,64,4,2048]{3,2,1,0:T(4,128)(2,1)} %copy.22) | data formatting | bytes 16777216 | tf_op jit(solution)/shard_map/all_to_all | solution.py:25
  915.9 0.0 copy-start.1
  915.9 43.0 %fusion = f32[8,64,4096]{2,1,0:T(8,128)} fusion(bf16[8,64,8192]{2,1,0:T(8,128)(2,1)} %all_to_all.33, bf16[4096,8192]{1,0:T(8,128)(2,1)} %param.7), kind=kOutput, calls=%fused_computation | convolution fusion | flops 34359738368 | bytes 83886080 | tf_op jit(solution)/shard_map/rti,si->rts/dot_general | solution.py:34
  958.9 0.0 reduce-scatter.2.cloned.1.call-update
  959.0 97.2 %reduce-scatter.2.cloned.1.call-done = f32[8,64,2048]{2,1,0:T(8,128)} async-done(((f32[8,64,4096]{2,1,0:T(8,128)}), f32[8,64,2048]{2,1,0:T(8,128)}) %reduce-scatter.2.cloned.1.call-update) | async-done | bytes 4194320 | tf_op jit(solution)/shard_map/reduce_scatter | solution.py:35
  1056.1 0.0 copy-done.1
Async XLA Ops:
  6.5 665.5 %copy-start = (bf16[256,256]{1,0:T(8,128)(2,1)S(1)}, bf16[256,256]{1,0:T(8,128)(2,1)}, u32[]{:S(2)}) copy-start(bf16[256,256]{1,0:T(8,128)(2,1)} %param.9) | copy-start | bytes 393220
  6.5 61.8 %all-gather.2.cloned.1.call-start = ((), (), s32[]{:S(2)}) async-start(), calls=%async_computation.3 | async-start | bytes 6291456 | tf_op jit(solution)/shard_map/all_gather | solution.py:12
  435.4 7.4 copy-start.2
  435.4 189.7 %all-to-all-start = ((bf16[4,2,524288]{2,1,0:T(2,128)(2,1)}), bf16[4,2,524288]{2,1,0:T(2,128)(2,1)}, u32[]{:S(2)}, u32[]{:S(2)}) async-start(bf16[4,2,524288]{2,1,0:T(2,128)(2,1)} %reshape.36), calls=%async_computation | async-start | bytes 16777216 | tf_op jit(solution)/shard_map/all_to_all | solution.py:20
  441.2 614.9 %reduce-scatter.2.cloned.1.call-start = ((), (), s32[]{:S(2)}) async-start(), calls=%async_computation.4 | async-start | bytes 12582912 | tf_op jit(solution)/shard_map/reduce_scatter | solution.py:35
  915.9 140.2 %copy-start.1 = (bf16[256,256]{1,0:T(8,128)(2,1)S(1)}, bf16[256,256]{1,0:T(8,128)(2,1)}, u32[]{:S(2)}) copy-start(bf16[256,256]{1,0:T(8,128)(2,1)} %param.9) | copy-start | bytes 393220
Sparse Core Ops, SparseCore 0:
  8.9 59.4 all-gather.1
  959.1 96.9 reduce-scatter.1
where the time goes:
time: 1060 us
  blocking collectives  475 us (45%)
  waiting for transfers between devices  341 us (32%)
  local copies, waits for them, and re-layouts  127 us (12%)
  matrix products  99.7 us (9%)
  between operations  14.1 us (1%)
    psum x1, blocking collectives, shards(): spectral = lax.psum(partial_value, 'row').astype(jnp.bfloat16)  288 us
    all_to_all x1, blocking collectives, shards(): lax.all_to_all(jnp.einsum('tj,kji->kti', time_basis, scaled, preferred_el...  187 us
    all_to_all x1, waiting for transfers between devices, shards(): lax.all_to_all(spectral, 'tm', split_axis=2, concat_axis=1, tiled=True)  182 us
    reduce_scatter x1, waiting for transfers between devices, shards(): return lax.psum_scatter(terms, 'col', scatter_dimension=2, tiled=True)  97.2 us
    all_gather x1, waiting for transfers between devices, shards(): lax.all_gather(right_sides, 'col', axis=2, tiled=True)  61.1 us
    dot_general x1, matrix products, shards(): jnp.einsum('rts,si->rti', lax.all_gather(right_sides, 'col', axis=2, tile...  44.2 us
    dot_general x1, matrix products, shards(): jnp.einsum('rti,si->rts', own_part, eigen_basis, preferred_element_type=j...  43 us
    unnamed x8, local copies, waits for them, and re-layouts  32.5 us
  transfers between devices with their start and end apart: 3, of which 3 were waited for; matrix products, arithmetic and copies ran while one was open for 0% of the time, Pallas kernels for 0%

commit v1 on v0

v1 whole, which is shorter than its diff:
```python
import functools

import jax
import jax.numpy as jnp
from jax import lax
from jax.experimental import pallas as pl
from jax.experimental.pallas import tpu as pltpu
from jax.sharding import PartitionSpec as P

BF16 = jnp.bfloat16
F32 = jnp.float32
PASSES = 2
MOST_PARTS = 8
LEAST_WIDE = 512
TILE = 256
STRIPS = 4
SEMS = 4
DEPTH = 6


def dot(a, b, dims):
    return lax.dot_general(a, b, (dims, ((), ())), preferred_element_type=F32)


def kernel(
    cols, tms, span, parts,
    noise, values, levels, basis, fields, eigen, out,
    sites, acc, e1, e2, near, core_out, core_in, mid, x_out, x_in, z_out, z_in,
    b_out, back, y_out, y_in,
    e1_sem, e2_sem, c1_s, c1_r, x1_s, x1_r, z1_s, z1_r, z2_s, z2_r, x2_s, x2_r, c2_s, c2_r,
    g_s, g_r, y_s, y_r,
):
    row, col, tm = lax.axis_index("row"), lax.axis_index("col"), lax.axis_index("tm")
    core, chip = lax.rem(row, 2), lax.div(row, 2)
    other_core = {"row": chip * 2 + (1 - core)}
    other_chip = {"row": (1 - chip) * 2 + core}
    lines = sites.shape[1]
    own = fields.shape[1]
    wide = back.shape[2]
    half, quarter = wide // 2, wide // 4
    strip = eigen.shape[0] // STRIPS
    count = PASSES * parts
    tiles = wide // TILE
    group = lines // tms

    def at(base, size):
        return pl.ds(pl.multiple_of(base, 128), size)

    def rows_at(base, size):
        return pl.ds(pl.multiple_of(base, 16), size)

    def remote(src, dst, send, recv, to):
        return pltpu.make_async_remote_copy(
            src_ref=src, dst_ref=dst, send_sem=send, recv_sem=recv,
            device_id=to, device_id_type=pl.DeviceIdType.MESH,
        )

    barrier = pltpu.get_barrier_semaphore()
    friends = [other_core, other_chip]
    friends += [{"tm": lax.rem(tm + d, tms)} for d in range(1, tms)]
    friends += [{"col": lax.rem(col + d, cols)} for d in range(1, cols)]
    for friend in friends:
        pl.semaphore_signal(barrier, inc=1, device_id=friend, device_id_type=pl.DeviceIdType.MESH)
    pl.semaphore_wait(barrier, len(friends))

    def gather(p, d):
        return remote(
            fields.at[pl.ds(p * lines, lines), :],
            sites.at[p, :, at(col * own, own)],
            g_s.at[p, d - 1], g_r.at[p, d - 1],
            {"col": lax.rem(col + d, cols)},
        )

    def scatter(p, d):
        return remote(
            y_out.at[p, d - 1], y_in.at[p, d - 1], y_s.at[p, d - 1], y_r.at[p, d - 1],
            {"col": lax.rem(col + d, cols)},
        )

    def c1(c):
        m = lax.rem(c, SEMS)
        return remote(core_out, core_in.at[c], c1_s.at[m], c1_r.at[m], other_core)

    def x1(c):
        m = lax.rem(c, SEMS)
        return remote(x_out, x_in.at[c], x1_s.at[m], x1_r.at[m], other_chip)

    def z1(c, d):
        m = lax.rem(c, SEMS)
        to = lax.rem(tm + d, tms)
        return remote(
            z_out.at[rows_at(to * group, group), :], z_in.at[c, tm],
            z1_s.at[m, d - 1], z1_r.at[m, d - 1], {"tm": to},
        )

    my_quarter = core * half + chip * quarter

    def z2(c, d):
        m = lax.rem(c, SEMS)
        to = lax.rem(tm + d, tms)
        return remote(
            b_out.at[to],
            back.at[c, rows_at(tm * group, group), at(my_quarter, quarter)],
            z2_s.at[m, d - 1], z2_r.at[m, d - 1], {"tm": to},
        )

    def x2(c):
        m = lax.rem(c, SEMS)
        place = back.at[c, :, at(my_quarter, quarter)]
        return remote(place, place, x2_s.at[m], x2_r.at[m], other_chip)

    def c2(c):
        m = lax.rem(c, SEMS)
        place = back.at[c, :, at(core * half, half)]
        return remote(place, place, c2_s.at[m], c2_r.at[m], other_core)

    def tile_start(j):
        per = tiles // 2
        side = (1 - core) if j < per else core
        return side * half + (j % per) * TILE

    def fetch1(c, j):
        first = lax.rem(c, parts) * wide + tile_start(j)
        return pltpu.make_async_copy(eigen.at[:, at(first, TILE)], e1.at[j % 2], e1_sem.at[j % 2])

    def fetch2(c, j):
        first = lax.rem(c, parts) * wide
        return pltpu.make_async_copy(
            eigen.at[pl.ds(j * strip, strip), at(first, wide)], e2.at[j % 2], e2_sem.at[j % 2]
        )

    for d in range(1, cols):
        gather(0, d).start()
    for p in range(PASSES):
        sites[p, :, at(col * own, own)] = fields[pl.ds(p * lines, lines), :]

    def step(s, carry):
        @pl.when(s < count)
        def _():
            fetch1(s, 0).start()
            fetch1(s, 1).start()

        @pl.when(s >= DEPTH)
        def _():
            fetch2(s - DEPTH, 0).start()
            fetch2(s - DEPTH, 1).start()

        @pl.when((s >= 5) & (s - 5 < count))
        def _():
            x2(s - 5).wait()
            c2(s - 5).start()

        @pl.when((s >= 4) & (s - 4 < count))
        def _():
            for d in range(1, tms):
                z2(s - 4, d).wait()
            x2(s - 4).start()

        @pl.when((s >= 3) & (s - 3 < count))
        def _():
            c = s - 3
            for d in range(1, tms):
                z1(c, d).wait()
            first = lax.rem(c, parts) * wide + my_quarter
            denom = levels[...] * values[:, at(first, quarter)] + noise[0]
            for r in range(group // span):
                lines_r = slice(r * span, (r + 1) * span)
                block = jnp.concatenate([z_in[c, j, lines_r, :] for j in range(tms)], axis=0)
                mixed = dot(basis[...], block, ((0,), (0,)))
                scaled = (mixed / denom).astype(BF16)
                result = dot(basis[...], scaled, ((1,), (0,))).astype(BF16)
                for j in range(tms):
                    b_out[j, lines_r, :] = result[j * span : (j + 1) * span, :]
            for d in range(1, tms):
                z2(c, d).start()
            back[c, rows_at(tm * group, group), at(my_quarter, quarter)] = b_out[tm]

        @pl.when((s >= 2) & (s - 2 < count))
        def _():
            c = s - 2
            x1(c).wait()
            z_out[...] = (mid[...] + x_in[c].astype(F32)).astype(BF16)
            for d in range(1, tms):
                z1(c, d).start()
            z_in[c, tm] = z_out[rows_at(tm * group, group), :]

        @pl.when((s >= 1) & (s - 1 < count))
        def _():
            c = s - 1
            c1(c).wait()
            far = at((1 - chip) * quarter, quarter)
            mine = at(chip * quarter, quarter)
            x_out[...] = (near[:, far] + core_in[c, :, far].astype(F32)).astype(BF16)
            x1(c).start()
            mid[...] = near[:, mine] + core_in[c, :, mine].astype(F32)

        @pl.when(s < count)
        def _():
            p = lax.div(s, parts)
            for q in range(PASSES):
                @pl.when(s == q * parts)
                def _():
                    for d in range(1, cols):
                        gather(q, d).wait()
                    if q + 1 < PASSES:
                        for d in range(1, cols):
                            gather(q + 1, d).start()

            for j in range(tiles):
                fetch1(s, j).wait()
                product = dot(sites[p], e1[j % 2], ((1,), (0,)))
                if j + 2 < tiles:
                    fetch1(s, j + 2).start()
                first = (j % (tiles // 2)) * TILE
                if j < tiles // 2:
                    core_out[:, first : first + TILE] = product.astype(BF16)
                else:
                    near[:, first : first + TILE] = product
                if j == tiles // 2 - 1:
                    c1(s).start()

        @pl.when(s >= DEPTH)
        def _():
            c = s - DEPTH
            c2(c).wait()

            @pl.when(lax.rem(c, parts) == 0)
            def _():
                acc[...] = jnp.zeros_like(acc)

            for j in range(STRIPS):
                fetch2(c, j).wait()
                acc[:, j * strip : (j + 1) * strip] += dot(back[c], e2[j % 2], ((1,), (1,)))
                if j + 2 < STRIPS:
                    fetch2(c, j + 2).start()
            for q in range(PASSES):
                @pl.when(c == (q + 1) * parts - 1)
                def _():
                    for d in range(1, cols):
                        to = lax.rem(col + d, cols)
                        y_out[q, d - 1] = acc[:, at(to * own, own)].astype(BF16)
                        scatter(q, d).start()
                    out[q * lines : (q + 1) * lines, :] = acc[:, at(col * own, own)]

        return carry

    lax.fori_loop(0, count + DEPTH, step, 0)
    for p in range(PASSES):
        for d in range(1, cols):
            scatter(p, d).wait()
            out[p * lines : (p + 1) * lines, :] += y_in[p, d - 1].astype(F32)


def shards(right_sides, eigen_basis, space_values, time_basis, time_values, noise_level):
    count, span, own = right_sides.shape
    cols, tms = lax.axis_size("col"), lax.axis_size("tm")
    lines = count * span // PASSES
    depth, width = eigen_basis.shape
    parts = min(MOST_PARTS, width // LEAST_WIDE)
    wide = width // parts
    half, quarter = wide // 2, wide // 4
    group = lines // tms
    chunks = PASSES * parts
    dma = pltpu.SemaphoreType.DMA
    vmem = pl.BlockSpec(memory_space=pltpu.VMEM)
    result = pl.pallas_call(
        functools.partial(kernel, cols, tms, span, parts),
        out_shape=jax.ShapeDtypeStruct((count * span, own), F32),
        in_specs=[pl.BlockSpec(memory_space=pltpu.SMEM), vmem, vmem, vmem, vmem]
        + [pl.BlockSpec(memory_space=pl.ANY)],
        out_specs=vmem,
        scratch_shapes=[
            pltpu.VMEM((PASSES, lines, depth), BF16),
            pltpu.VMEM((lines, depth), F32),
            pltpu.VMEM((2, depth, TILE), BF16),
            pltpu.VMEM((2, depth // STRIPS, wide), BF16),
            pltpu.VMEM((lines, half), F32),
            pltpu.VMEM((lines, half), BF16),
            pltpu.VMEM((chunks, lines, half), BF16),
            pltpu.VMEM((lines, quarter), F32),
            pltpu.VMEM((lines, quarter), BF16),
            pltpu.VMEM((chunks, lines, quarter), BF16),
            pltpu.VMEM((lines, quarter), BF16),
            pltpu.VMEM((chunks, tms, group, quarter), BF16),
            pltpu.VMEM((tms, group, quarter), BF16),
            pltpu.VMEM((chunks, lines, wide), BF16),
            pltpu.VMEM((PASSES, cols - 1, lines, own), BF16),
            pltpu.VMEM((PASSES, cols - 1, lines, own), BF16),
            dma((2,)), dma((2,)),
            dma((SEMS,)), dma((SEMS,)), dma((SEMS,)), dma((SEMS,)),
            dma((SEMS, tms - 1)), dma((SEMS, tms - 1)),
            dma((SEMS, tms - 1)), dma((SEMS, tms - 1)),
            dma((SEMS,)), dma((SEMS,)), dma((SEMS,)), dma((SEMS,)),
            dma((PASSES, cols - 1)), dma((PASSES, cols - 1)),
            dma((PASSES, cols - 1)), dma((PASSES, cols - 1)),
        ],
        compiler_params=pltpu.CompilerParams(
            collective_id=0, has_side_effects=True, vmem_limit_bytes=60 * 1024 * 1024
        ),
        cost_estimate=pl.CostEstimate(
            flops=4 * count * span * depth * width,
            bytes_accessed=4 * PASSES * depth * width,
            transcendentals=0,
        ),
    )(
        noise_level, space_values.reshape(1, -1), time_values.reshape(-1, 1), time_basis,
        right_sides.reshape(count * span, own), eigen_basis,
    )
    return result.reshape(count, span, own)


def solution(mesh):
    placed = (P(None, "tm", ("row", "col")), P("row", "col"), P("col"), P(), P(), P())
    return jax.shard_map(
        shards, mesh=mesh, in_specs=placed, out_specs=P(None, "tm", ("row", "col")), check_vma=False
    )
```

time: 1060 us -> 242 us (0.23)
  blocking collectives: 475 us -> 0 us
  waiting for transfers between devices: 341 us -> 0 us
  Pallas kernels: 0 us -> 234 us
  local copies, waits for them, and re-layouts: 127 us -> 6.17 us
  matrix products: 99.7 us -> 0 us
  between operations: 14.1 us -> 0.66 us
    psum x1 -> x0, blocking collectives: 288 us -> none  [shards(): spectral = lax.psum(partial_value, 'row').astype(jnp.bfloat16)]
    pallas_call x0 -> x1, Pallas kernels: none -> 234 us  [shards(): pl.pallas_call(functools.partial(kernel, cols, tms, span, parts), out_sha...]
    all_to_all x1 -> x0, blocking collectives: 187 us -> none  [shards(): lax.all_to_all(jnp.einsum('tj,kji->kti', time_basis, scaled, preferred_el...]
    all_to_all x1 -> x0, waiting for transfers between devices: 182 us -> none  [shards(): lax.all_to_all(spectral, 'tm', split_axis=2, concat_axis=1, tiled=True)]
    dot_general x3 -> x0, matrix products: 99.7 us -> none  [the longest x1 44.2 us: shards(): jnp.einsum('rts,si->rti', lax.all_gather(right_sides, 'col', axis=2, tile...]
    reduce_scatter x1 -> x0, waiting for transfers between devices: 97.2 us -> none  [shards(): return lax.psum_scatter(terms, 'col', scatter_dimension=2, tiled=True)]
    all_to_all x4 -> x0, local copies, waits for them, and re-layouts: 62.7 us -> none  [the longest x2 31.7 us: shards(): lax.all_to_all(jnp.einsum('tj,kji->kti', time_basis, scaled, preferred_el...]
    all_gather x1 -> x0, waiting for transfers between devices: 61.1 us -> none  [shards(): lax.all_gather(right_sides, 'col', axis=2, tiled=True)]
  transfers between devices with their start and end apart: 3 -> 0, of which waited for: 3 -> 0; matrix products, arithmetic and copies ran while one was open for 0% -> 0% of each run, Pallas kernels for 0% -> 0%
where the time goes in v1:
time: 242 us; the launch traced here: 241 us
  Pallas kernels  234 us (97%)
  local copies, waits for them, and re-layouts  6.17 us (3%)
    pallas_call x1, Pallas kernels, shards(): pl.pallas_call(functools.partial(kernel, cols, tms, span, parts), out_sha...  234 us

profile of v1, /device:TPU:0, one launch (start us, length us, event | category | flops | bytes accessed | tf_op | source)
XLA Modules:
  0.0 241.0 jit_solution(12461735795535715548)
XLA Ops:
  0.7 1.5 copy.7.levels
  2.1 234.2 %shard_map.64 = f32[512,2048]{1,0:T(8,128)} custom-call(f32[1]{0:T(128)S(6)} %copy.9.noise, f32[1,8192]{1,0:T(1,128)} %bitcast.7, f32[256,1]{1,0:T(8,128)} %copy.7.levels, bf16[256,256]{1,0:T(8,128)(2,1)} %basis.1, bf16[512,2048]{1,0:T(8,128)(2,1)} %bitcast.6, bf16[4096,8192]{1,0:T(8,128)(2,1)} %eigen.1), custom_call_target="tpu_custom_call" | custom-call | flops 68719476736 | bytes 268435456 | tf_op jit(solution)/shard_map/pallas_call | solution.py:266
  236.3 4.7 %copy.10 = f32[8,64,2048]{2,1,0:T(8,128)} copy(f32[8,64,2048]{2,1,0:T(8,128)} %bitcast.4) | data formatting | bytes 8388608

commit v2 on v1

--- a/solution.py
+++ b/solution.py
@@ -13,7 +13,7 @@
 MOST_PARTS = 8
 LEAST_WIDE = 512
 TILE = 256
-STRIPS = 4
+STRIP = 1024
 SEMS = 4
 DEPTH = 6
 
@@ -25,7 +25,7 @@
 def kernel(
     cols, tms, span, parts,
     noise, values, levels, basis, fields, eigen, out,
-    sites, acc, e1, e2, near, core_out, core_in, mid, x_out, x_in, z_out, z_in,
+    sites, pre, acc, e1, e2, near, core_out, core_in, mid, x_out, x_in, z_out, z_in,
     b_out, back, y_out, y_in,
     e1_sem, e2_sem, c1_s, c1_r, x1_s, x1_r, z1_s, z1_r, z2_s, z2_r, x2_s, x2_r, c2_s, c2_r,
     g_s, g_r, y_s, y_r,
@@ -34,11 +34,12 @@
     core, chip = lax.rem(row, 2), lax.div(row, 2)
     other_core = {"row": chip * 2 + (1 - core)}
     other_chip = {"row": (1 - chip) * 2 + core}
-    lines = sites.shape[1]
+    lines = acc.shape[0]
     own = fields.shape[1]
     wide = back.shape[2]
     half, quarter = wide // 2, wide // 4
-    strip = eigen.shape[0] // STRIPS
+    strip = e2.shape[1]
+    strips = own // strip
     count = PASSES * parts
     tiles = wide // TILE
     group = lines // tms
@@ -66,7 +67,7 @@
     def gather(p, d):
         return remote(
             fields.at[pl.ds(p * lines, lines), :],
-            sites.at[p, :, at(col * own, own)],
+            sites.at[p, d - 1],
             g_s.at[p, d - 1], g_r.at[p, d - 1],
             {"col": lax.rem(col + d, cols)},
         )
@@ -119,31 +120,91 @@
         side = (1 - core) if j < per else core
         return side * half + (j % per) * TILE
 
-    def fetch1(c, j):
+    def fetch1(c, j, d):
         first = lax.rem(c, parts) * wide + tile_start(j)
-        return pltpu.make_async_copy(eigen.at[:, at(first, TILE)], e1.at[j % 2], e1_sem.at[j % 2])
+        block = lax.rem(col - d + cols, cols)
+        return pltpu.make_async_copy(
+            eigen.at[rows_at(block * own, own), at(first, TILE)],
+            e1.at[j % 2, d], e1_sem.at[j % 2, d],
+        )
 
     def fetch2(c, j):
         first = lax.rem(c, parts) * wide
+        block = lax.rem(col + 1 + j // strips, cols)
         return pltpu.make_async_copy(
-            eigen.at[pl.ds(j * strip, strip), at(first, wide)], e2.at[j % 2], e2_sem.at[j % 2]
-        )
+            eigen.at[rows_at(block * own + (j % strips) * strip, strip), at(first, wide)],
+            e2.at[j % 2], e2_sem.at[j % 2],
+        )
+
+    def fetch_head(t):
+        slot = lax.rem(t, 2)
+        return pltpu.make_async_copy(
+            eigen.at[rows_at(col * own, own), at(t * TILE, TILE)],
+            e1.at[slot, 0], e1_sem.at[slot, 0],
+        )
+
+    def fetch_tail(t):
+        slot = lax.rem(t, 2)
+        k, i = lax.div(t, strips), lax.rem(t, strips)
+        return pltpu.make_async_copy(
+            eigen.at[rows_at(col * own + i * strip, strip), at(k * wide, wide)],
+            e2.at[slot], e2_sem.at[slot],
+        )
+
+    heads, tails = parts * tiles, parts * strips
 
     for d in range(1, cols):
         gather(0, d).start()
-    for p in range(PASSES):
-        sites[p, :, at(col * own, own)] = fields[pl.ds(p * lines, lines), :]
+    fetch_head(0).start()
+    fetch_head(1).start()
+
+    def head(t, carry):
+        fetch_head(t).wait()
+        pre[:, at(t * TILE, TILE)] = dot(fields[0:lines, :], e1[lax.rem(t, 2), 0], ((1,), (0,)))
+
+        @pl.when(t + 2 < heads)
+        def _():
+            fetch_head(t + 2).start()
+
+        return carry
+
+    lax.fori_loop(0, heads, head, 0)
+    others = (cols - 1) * strips
+
+    def project(s, q):
+        lo = 1 if q == 0 else 0
+        for j in range(tiles):
+            product = None
+            if q == 0:
+                product = pre[:, at(lax.rem(s, parts) * wide + tile_start(j), TILE)]
+            for d in range(lo, cols):
+                fetch1(s, j, d).wait()
+                left = fields[q * lines : (q + 1) * lines, :] if d == 0 else sites[q, d - 1]
+                term = dot(left, e1[j % 2, d], ((1,), (0,)))
+                product = term if product is None else product + term
+            if j + 2 < tiles:
+                for d in range(lo, cols):
+                    fetch1(s, j + 2, d).start()
+            first = (j % (tiles // 2)) * TILE
+            if j < tiles // 2:
+                core_out[:, first : first + TILE] = product.astype(BF16)
+            else:
+                near[:, first : first + TILE] = product
+            if j == tiles // 2 - 1:
+                c1(s).start()
 
     def step(s, carry):
-        @pl.when(s < count)
-        def _():
-            fetch1(s, 0).start()
-            fetch1(s, 1).start()
+        for q in range(PASSES):
+            @pl.when((s >= q * parts) & (s < (q + 1) * parts))
+            def _():
+                for j in range(2):
+                    for d in range(1 if q == 0 else 0, cols):
+                        fetch1(s, j, d).start()
 
         @pl.when(s >= DEPTH)
         def _():
-            fetch2(s - DEPTH, 0).start()
-            fetch2(s - DEPTH, 1).start()
+            for j in range(min(2, others)):
+                fetch2(s - DEPTH, j).start()
 
         @pl.when((s >= 5) & (s - 5 < count))
         def _():
@@ -194,30 +255,18 @@
             x1(c).start()
             mid[...] = near[:, mine] + core_in[c, :, mine].astype(F32)
 
-        @pl.when(s < count)
-        def _():
-            p = lax.div(s, parts)
-            for q in range(PASSES):
-                @pl.when(s == q * parts)
-                def _():
+        for q in range(PASSES):
+            @pl.when(s == q * parts)
+            def _():
+                for d in range(1, cols):
+                    gather(q, d).wait()
+                if q + 1 < PASSES:
                     for d in range(1, cols):
-                        gather(q, d).wait()
-                    if q + 1 < PASSES:
-                        for d in range(1, cols):
-                            gather(q + 1, d).start()
-
-            for j in range(tiles):
-                fetch1(s, j).wait()
-                product = dot(sites[p], e1[j % 2], ((1,), (0,)))
-                if j + 2 < tiles:
-                    fetch1(s, j + 2).start()
-                first = (j % (tiles // 2)) * TILE
-                if j < tiles // 2:
-                    core_out[:, first : first + TILE] = product.astype(BF16)
-                else:
-                    near[:, first : first + TILE] = product
-                if j == tiles // 2 - 1:
-                    c1(s).start()
+                        gather(q + 1, d).start()
+
+            @pl.when((s >= q * parts) & (s < (q + 1) * parts))
+            def _():
+                project(s, q)
 
         @pl.when(s >= DEPTH)
         def _():
@@ -228,23 +277,40 @@
             def _():
                 acc[...] = jnp.zeros_like(acc)
 
-            for j in range(STRIPS):
+            for j in range(others):
                 fetch2(c, j).wait()
                 acc[:, j * strip : (j + 1) * strip] += dot(back[c], e2[j % 2], ((1,), (1,)))
-                if j + 2 < STRIPS:
+                if j + 2 < others:
                     fetch2(c, j + 2).start()
             for q in range(PASSES):
                 @pl.when(c == (q + 1) * parts - 1)
                 def _():
                     for d in range(1, cols):
-                        to = lax.rem(col + d, cols)
-                        y_out[q, d - 1] = acc[:, at(to * own, own)].astype(BF16)
+                        y_out[q, d - 1] = acc[:, (d - 1) * own : d * own].astype(BF16)
                         scatter(q, d).start()
-                    out[q * lines : (q + 1) * lines, :] = acc[:, at(col * own, own)]
 
         return carry
 
     lax.fori_loop(0, count + DEPTH, step, 0)
+    fetch_tail(0).start()
+    fetch_tail(1).start()
+    out[...] = jnp.zeros_like(out)
+
+    def tail(t, carry):
+        fetch_tail(t).wait()
+        k, i = lax.div(t, strips), lax.rem(t, strips)
+        tile = e2[lax.rem(t, 2)]
+        place = at(i * strip, strip)
+        for p in range(PASSES):
+            out[p * lines : (p + 1) * lines, place] += dot(back[p * parts + k], tile, ((1,), (1,)))
+
+        @pl.when(t + 2 < tails)
+        def _():
+            fetch_tail(t + 2).start()
+
+        return carry
+
+    lax.fori_loop(0, tails, tail, 0)
     for p in range(PASSES):
         for d in range(1, cols):
             scatter(p, d).wait()
@@ -270,10 +336,11 @@
         + [pl.BlockSpec(memory_space=pl.ANY)],
         out_specs=vmem,
         scratch_shapes=[
-            pltpu.VMEM((PASSES, lines, depth), BF16),
-            pltpu.VMEM((lines, depth), F32),
-            pltpu.VMEM((2, depth, TILE), BF16),
-            pltpu.VMEM((2, depth // STRIPS, wide), BF16),
+            pltpu.VMEM((PASSES, cols - 1, lines, own), BF16),
+            pltpu.VMEM((lines, width), F32),
+            pltpu.VMEM((lines, (cols - 1) * own), F32),
+            pltpu.VMEM((2, cols, own, TILE), BF16),
+            pltpu.VMEM((2, min(STRIP, own), wide), BF16),
             pltpu.VMEM((lines, half), F32),
             pltpu.VMEM((lines, half), BF16),
             pltpu.VMEM((chunks, lines, half), BF16),
@@ -286,7 +353,7 @@
             pltpu.VMEM((chunks, lines, wide), BF16),
             pltpu.VMEM((PASSES, cols - 1, lines, own), BF16),
             pltpu.VMEM((PASSES, cols - 1, lines, own), BF16),
-            dma((2,)), dma((2,)),
+            dma((2, cols)), dma((2,)),
             dma((SEMS,)), dma((SEMS,)), dma((SEMS,)), dma((SEMS,)),
             dma((SEMS, tms - 1)), dma((SEMS, tms - 1)),
             dma((SEMS, tms - 1)), dma((SEMS, tms - 1)),

time: 242 us -> 213 us (0.88)
  Pallas kernels: 234 us -> 205 us
    pallas_call x1, Pallas kernels: 234 us -> 205 us  [shards(): pl.pallas_call(functools.partial(kernel, cols, tms, span, parts), out_sha...]
where the time goes in v2:
time: 213 us; the launch traced here: 212 us
  Pallas kernels  205 us (96%)
  local copies, waits for them, and re-layouts  6.17 us (3%)
    pallas_call x1, Pallas kernels, shards(): pl.pallas_call(functools.partial(kernel, cols, tms, span, parts), out_sha...  205 us
    unnamed x1, local copies, waits for them, and re-layouts  4.7 us

profile of v2, /device:TPU:0, one launch (start us, length us, event | category | flops | bytes accessed | tf_op | source)
XLA Modules:
  0.0 211.7 jit_solution(11480357587781194883)
XLA Ops:
  0.7 1.5 copy.7.levels
  2.1 204.8 %shard_map.64 = f32[512,2048]{1,0:T(8,128)} custom-call(f32[1]{0:T(128)S(6)} %copy.9.noise, f32[1,8192]{1,0:T(1,128)} %bitcast.7, f32[256,1]{1,0:T(8,128)} %copy.7.levels, bf16[256,256]{1,0:T(8,128)(2,1)} %basis.1, bf16[512,2048]{1,0:T(8,128)(2,1)} %bitcast.6, bf16[4096,8192]{1,0:T(8,128)(2,1)} %eigen.1), custom_call_target="tpu_custom_call" | custom-call | flops 68719476736 | bytes 268435456 | tf_op jit(solution)/shard_map/pallas_call | solution.py:332
  207.0 4.7 %copy.10 = f32[8,64,2048]{2,1,0:T(8,128)} copy(f32[8,64,2048]{2,1,0:T(8,128)} %bitcast.4) | data formatting | bytes 8388608
